TPU v7x, 256 devices: a whole 4x4x8 slice. The times are simulated.
256 devices in a mesh: span: 4 (over x), seq: 32 (over z, y), tp: 2 (over core).
Axes of the slice: x: 4, y: 4, z: 8, core: 2. Of those that a mesh axis runs over, the one named last changes fastest.
Arguments:
- query_states: bfloat16 [4, 3072, 4096], P('span', ('seq', 'tp')), may hold values from -8 to 8
- key_states: bfloat16 [4, 3072, 4096], P('span', ('seq', 'tp')), may hold values from -8 to 8
- value_states: bfloat16 [4, 3072, 4096], P('span', ('seq', 'tp')), may hold values from -6 to 6
- frame_mask: int32 [4, 96], replicated, may hold values from 0 to 1, as said below
- levels: int32 [4], P('span'), may hold values from 0 to 15
- gate_table: float32 [16, 4096], replicated, may hold values from 0.1 to 1.9
Outputs:
- gated_out: bfloat16 [4, 3072, 4096], P('span', ('seq', 'tp'))
Inputs may be any that keep to these rules, and one draw needn't show every extreme that they name: frame_mask[c, f] is 1 for every frame f of span c and 0 for every frame of later spans.
All inputs are finite; a program needn't handle non-finite values.
Results may differ from a plain program's by a relative error of at most 0.006.
Values may be sent and summed in bfloat16 or wider, within the bound.
A program may use at most 128 MiB of HBM per device.

v0:
```python
import functools
import math

import jax
import jax.numpy as jnp
from jax import lax
from jax.experimental import pallas as pl
from jax.experimental.pallas import tpu as pltpu
from jax.sharding import PartitionSpec as P

MESH = pl.DeviceIdType.MESH
HEAD = 128
SPANS = 4
NX, NY, NZ = 4, 4, 8
ROWS = 48
FRAMES = 24
QROWS = NZ * ROWS
FEATURES = NX * NZ * HEAD
LOG2_SCALE = math.log2(math.e) / math.sqrt(HEAD)
NEG = -1e30
K, V, Q = 0, 1, 2


def body(
    levels, mask, q_in, k_in, v_in, gate, out,
    kbuf, vbuf, qbuf, sbuf, mine, merged,
    a2a_send, a2a_recv, y_send, y_recv, c_send, c_recv, o_send, o_recv,
):
    x = lax.axis_index("span")
    s = lax.axis_index("seq")
    c = lax.axis_index("tp")
    y, z = s % NY, s // NY
    up, down, far = (y + 1) % NY, (y + NY - 1) % NY, (y + 2) % NY
    head = x * NZ + z

    def peer(i):
        return (x + i // NZ) % NX, (z + i % NZ) % NZ

    barrier = pltpu.get_barrier_semaphore()

    def greet(i, carry):
        px, pz = peer(i)
        pl.semaphore_signal(barrier, inc=1, device_id=(px, pz * NY + y, c), device_id_type=MESH)
        return carry

    lax.fori_loop(1, NX * NZ, greet, 0)
    for to in ((x, z * NY + up, c), (x, z * NY + down, c), (x, s, 1 - c)):
        pl.semaphore_signal(barrier, inc=1, device_id=to, device_id_type=MESH)

    for span in range(SPANS):
        vbuf[span, :, :, :, HEAD:] = jnp.ones((NZ, NY * 2, ROWS, HEAD), jnp.bfloat16)

    pl.semaphore_wait(barrier, NX * NZ - 1 + 3)

    def cols(h):
        return pl.ds(pl.multiple_of(h * HEAD, HEAD), HEAD)

    srcs = (k_in, v_in, q_in)

    def block(arr, span, zs, who):
        if arr == Q:
            return qbuf.at[span, zs]
        if arr == K:
            return kbuf.at[span, zs, who]
        return vbuf.at[span, zs, who, :, pl.ds(0, HEAD)]

    whole, low, high = pl.ds(0, NZ), pl.ds(0, NZ // 2), pl.ds(NZ // 2, NZ // 2)
    me = y * 2 + c
    lo, hi, across = down * 2 + c, up * 2 + c, far * 2 + c

    def issue(arr):
        pltpu.make_async_copy(srcs[arr].at[:, cols(head)], block(arr, x, z, me), a2a_recv.at[arr, x]).start()

        def one(i, carry):
            px, pz = peer(i)
            pltpu.make_async_remote_copy(
                src_ref=srcs[arr].at[:, cols(px * NZ + pz)],
                dst_ref=block(arr, x, z, me),
                send_sem=a2a_send.at[arr],
                recv_sem=a2a_recv.at[arr, x],
                device_id=(px, pz * NY + y, c),
                device_id_type=MESH,
            ).start()
            return carry

        lax.fori_loop(1, NX * NZ, one, 0)

    def arrived(arr, span):
        b = block(arr, span, whole, me)
        pltpu.make_async_copy(b, b, a2a_recv.at[arr, span]).wait()

    def y_copy(arr, span, zs, who, to, kind):
        b = block(arr, span, zs, who)
        return pltpu.make_async_remote_copy(
            src_ref=b, dst_ref=b, send_sem=y_send.at[arr, span, kind], recv_sem=y_recv.at[arr, span, kind],
            device_id=(x, z * NY + to, c), device_id_type=MESH)

    def c_copy(arr, span, zs, who, kind):
        b = block(arr, span, zs, who)
        return pltpu.make_async_remote_copy(
            src_ref=b, dst_ref=b, send_sem=c_send.at[arr, span, kind], recv_sem=c_recv.at[arr, span, kind],
            device_id=(x, s, 1 - c), device_id_type=MESH)

    def share(arr, span):
        arrived(arr, span)
        y_copy(arr, span, whole, me, up, 0).start()
        y_copy(arr, span, whole, me, down, 1).start()
        c_copy(arr, span, whole, me, 0).start()

    def forward(arr, span):
        y_copy(arr, span, whole, lo, up, 0).wait_recv()
        y_copy(arr, span, low, lo, up, 2).start()
        c_copy(arr, span, whole, lo, 1).start()
        y_copy(arr, span, whole, hi, down, 1).wait_recv()
        y_copy(arr, span, high, hi, down, 3).start()
        c_copy(arr, span, whole, hi, 2).start()

    def finish(arr, span):
        y_copy(arr, span, low, across, up, 2).wait_recv()
        c_copy(arr, span, low, across, 3).start()
        y_copy(arr, span, high, across, down, 3).wait_recv()
        c_copy(arr, span, high, across, 4).start()

    def collect(arr, span):
        for kind, zs in enumerate((whole, whole, whole, low, high)):
            c_copy(arr, span, zs, me, kind).wait_recv()

    issue(K)
    issue(V)
    todo = [(arr, (x + NX - i) % NX) for arr in (K, V) for i in range(NX)]
    for n in range(len(todo) + 3):
        if n == 3:
            issue(Q)
        if n < len(todo):
            share(*todo[n])
        if 0 <= n - 1 < len(todo):
            forward(*todo[n - 1])
        if 0 <= n - 2 < len(todo):
            finish(*todo[n - 2])
        if 0 <= n - 3 < len(todo):
            collect(*todo[n - 3])

    def score(own, span, mx, masked):
        keys = kbuf[span].reshape(FRAMES * HEAD, HEAD)
        sc = lax.dot_general(
            qbuf[own].reshape(QROWS, HEAD), keys, (((1,), (1,)), ((), ())), preferred_element_type=jnp.float32)
        for f in range(FRAMES):
            part = sc[:, f * HEAD : (f + 1) * HEAD]
            if masked:
                part = part + jnp.where(mask[own, span * FRAMES + f] > 0, 0.0, NEG).astype(jnp.float32)
            sbuf[span * FRAMES + f] = part
            mx = jnp.maximum(mx, part)
        return mx

    def weigh(span, top, total):
        parts = [
            jnp.exp2(sbuf[span * FRAMES + f] * LOG2_SCALE - top).astype(jnp.bfloat16) for f in range(FRAMES)
        ]
        values = vbuf[span].reshape(FRAMES * HEAD, 2 * HEAD)
        return total + jnp.dot(jnp.concatenate(parts, axis=1), values, preferred_element_type=jnp.float32)

    def give(own, dz):
        pz = (z + dz) % NZ
        return pltpu.make_async_remote_copy(
            src_ref=mine.at[own, pz], dst_ref=merged.at[:, cols(head)], send_sem=o_send, recv_sem=o_recv,
            device_id=(own, pz * NY + y, c), device_id_type=MESH)

    for own in range(SPANS):
        arrived(Q, own)
        mx = jnp.full((QROWS, HEAD), NEG, jnp.float32)
        mx = score(own, own, mx, False)
        if own:
            mx = lax.fori_loop(0, own, lambda i, cur: score(own, i, cur, True), mx)
        top = jnp.broadcast_to(jnp.max(mx, axis=1, keepdims=True) * LOG2_SCALE, (QROWS, HEAD))
        total = lax.fori_loop(
            0, own + 1, lambda i, cur: weigh(i, top, cur), jnp.zeros((QROWS, 2 * HEAD), jnp.float32))
        result = (total[:, :HEAD] / total[:, HEAD:]).astype(jnp.bfloat16)
        mine[own] = result.reshape(NZ, ROWS, HEAD)
        for dz in range(1, NZ):
            give(own, dz).start()

        @pl.when(x != own)
        def _():
            give(own, 0).start()

        @pl.when(x == own)
        def _():
            pltpu.make_async_copy(mine.at[own, z], merged.at[:, cols(head)], o_recv).start()

    row = gate[pl.ds(levels[0], 1), :]
    pltpu.make_async_copy(merged, merged, o_recv).wait()
    out[...] = (row * merged[...].astype(jnp.float32)).astype(jnp.bfloat16)

    part = merged.at[:, pl.ds(0, FEATURES - HEAD)]
    pltpu.make_async_copy(part, part, o_send).wait()
    for arr in (K, V, Q):
        part = srcs[arr].at[:, pl.ds(0, FEATURES - HEAD)]
        pltpu.make_async_copy(part, part, a2a_send.at[arr]).wait()
    for arr, span in todo:
        for kind, zs in enumerate((whole, whole, low, high)):
            y_copy(arr, span, zs, me, up, kind).wait_send()
        for kind, zs in enumerate((whole, whole, whole, low, high)):
            c_copy(arr, span, zs, me, kind).wait_send()


def on_device(query_states, key_states, value_states, frame_mask, levels, gate_table):
    bf16 = jnp.bfloat16
    hbm = pl.BlockSpec(memory_space=pl.ANY)
    smem = pl.BlockSpec(memory_space=pltpu.SMEM)
    vmem = pl.BlockSpec(memory_space=pltpu.VMEM)
    dma = pltpu.SemaphoreType.DMA
    result = pl.pallas_call(
        body,
        out_shape=jax.ShapeDtypeStruct((ROWS, FEATURES), bf16),
        in_specs=[smem, smem, hbm, hbm, hbm, vmem],
        out_specs=vmem,
        scratch_shapes=[
            pltpu.VMEM((SPANS, NZ, NY * 2, ROWS, HEAD), bf16),
            pltpu.VMEM((SPANS, NZ, NY * 2, ROWS, 2 * HEAD), bf16),
            pltpu.VMEM((SPANS, NZ, ROWS, HEAD), bf16),
            pltpu.VMEM((SPANS * FRAMES, QROWS, HEAD), jnp.float32),
            pltpu.VMEM((SPANS, NZ, ROWS, HEAD), bf16),
            pltpu.VMEM((ROWS, FEATURES), bf16),
            dma((3,)),
            dma((3, SPANS)),
            dma((2, SPANS, 4)),
            dma((2, SPANS, 4)),
            dma((2, SPANS, 5)),
            dma((2, SPANS, 5)),
            dma,
            dma,
        ],
        compiler_params=pltpu.CompilerParams(
            collective_id=0, has_side_effects=True, vmem_limit_bytes=56 * 2**20
        ),
    )(levels, frame_mask, query_states[0], key_states[0], value_states[0], gate_table)
    return result[None]


def solution(mesh):
    split = P("span", ("seq", "tp"), None)
    return jax.shard_map(
        on_device,
        mesh=mesh,
        in_specs=(split, split, split, P(), P("span"), P()),
        out_specs=split,
        check_vma=False,
    )
```

profile of v0, /device:TPU:6, one launch (start us, length us, event | category | flops | bytes accessed | tf_op | source)
XLA Modules:
  0.0 76.9 jit_solution(11967976810668412256)
XLA Ops:
  0.7 74.5 %shard_map.64 = bf16[48,4096]{1,0:T(8,128)(2,1)} custom-call(s32[1]{0:T(128)S(6)} %copy.8.levels, s32[4,96]{1,0:T(4,128)} %mask.1, bf16[48,4096]{1,0:T(8,128)(2,1)} %bitcast.5, bf16[48,4096]{1,0:T(8,128)(2,1)} %bitcast.6, bf16[48,4096]{1,0:T(8,128)(2,1)} %bitcast.7, f32[16,4096]{1,0:T(8,128)} %gate.1), custom_call_target="tpu_custom_call" | custom-call | tf_op jit(solution)/shard_map/pallas_call | solution.py:212
  75.1 1.8 %copy.9 = bf16[1,48,4096]{2,1,0:T(8,128)(2,1)} copy(bf16[1,48,4096]{2,1,0:T(8,128)(2,1)} %bitcast.4) | data formatting | bytes 786432
where the time goes:
time: 77.9 us; the launch traced here: 76.9 us
  Pallas kernels  74.5 us (96%)
  local copies, waits for them, and re-layouts  1.77 us (2%)
    pallas_call x1, Pallas kernels, on_device(): pl.pallas_call(body, out_shape=jax.ShapeDtypeStruct((ROWS, FEATURES), bf1...  74.5 us
    unnamed x1, local copies, waits for them, and re-layouts  1.77 us

commit v1 on v0

--- a/solution.py
+++ b/solution.py
@@ -23,7 +23,7 @@
 
 def body(
     levels, mask, q_in, k_in, v_in, gate, out,
-    kbuf, vbuf, qbuf, sbuf, mine, merged,
+    kbuf, vbuf, qbuf, sbuf, peak, mine, merged,
     a2a_send, a2a_recv, y_send, y_recv, c_send, c_recv, o_send, o_recv,
 ):
     x = lax.axis_index("span")
@@ -68,8 +68,9 @@
     me = y * 2 + c
     lo, hi, across = down * 2 + c, up * 2 + c, far * 2 + c
 
-    def issue(arr):
-        pltpu.make_async_copy(srcs[arr].at[:, cols(head)], block(arr, x, z, me), a2a_recv.at[arr, x]).start()
+    def issue(arr, start=0, stop=NX):
+        if start == 0:
+            pltpu.make_async_copy(srcs[arr].at[:, cols(head)], block(arr, x, z, me), a2a_recv.at[arr, x]).start()
 
         def one(i, carry):
             px, pz = peer(i)
@@ -83,7 +84,7 @@
             ).start()
             return carry
 
-        lax.fori_loop(1, NX * NZ, one, 0)
+        lax.fori_loop(max(1, start * NZ), stop * NZ, one, 0)
 
     def arrived(arr, span):
         b = block(arr, span, whole, me)
@@ -125,36 +126,25 @@
         for kind, zs in enumerate((whole, whole, whole, low, high)):
             c_copy(arr, span, zs, me, kind).wait_recv()
 
-    issue(K)
-    issue(V)
-    todo = [(arr, (x + NX - i) % NX) for arr in (K, V) for i in range(NX)]
-    for n in range(len(todo) + 3):
-        if n == 3:
-            issue(Q)
-        if n < len(todo):
-            share(*todo[n])
-        if 0 <= n - 1 < len(todo):
-            forward(*todo[n - 1])
-        if 0 <= n - 2 < len(todo):
-            finish(*todo[n - 2])
-        if 0 <= n - 3 < len(todo):
-            collect(*todo[n - 3])
-
-    def score(own, span, mx, masked):
+    def unit(own, span):
+        return (own * (own + 1) // 2 + span) * FRAMES
+
+    def score(own, span, masked):
         keys = kbuf[span].reshape(FRAMES * HEAD, HEAD)
         sc = lax.dot_general(
             qbuf[own].reshape(QROWS, HEAD), keys, (((1,), (1,)), ((), ())), preferred_element_type=jnp.float32)
+        mx = None if span is own else peak[own]
         for f in range(FRAMES):
             part = sc[:, f * HEAD : (f + 1) * HEAD]
             if masked:
                 part = part + jnp.where(mask[own, span * FRAMES + f] > 0, 0.0, NEG).astype(jnp.float32)
-            sbuf[span * FRAMES + f] = part
-            mx = jnp.maximum(mx, part)
-        return mx
-
-    def weigh(span, top, total):
+            sbuf[unit(own, span) + f] = part
+            mx = part if mx is None else jnp.maximum(mx, part)
+        peak[own] = mx
+
+    def weigh(own, span, top, total):
         parts = [
-            jnp.exp2(sbuf[span * FRAMES + f] * LOG2_SCALE - top).astype(jnp.bfloat16) for f in range(FRAMES)
+            jnp.exp2(sbuf[unit(own, span) + f] * LOG2_SCALE - top).astype(jnp.bfloat16) for f in range(FRAMES)
         ]
         values = vbuf[span].reshape(FRAMES * HEAD, 2 * HEAD)
         return total + jnp.dot(jnp.concatenate(parts, axis=1), values, preferred_element_type=jnp.float32)
@@ -165,15 +155,43 @@
             src_ref=mine.at[own, pz], dst_ref=merged.at[:, cols(head)], send_sem=o_send, recv_sem=o_recv,
             device_id=(own, pz * NY + y, c), device_id_type=MESH)
 
-    for own in range(SPANS):
-        arrived(Q, own)
-        mx = jnp.full((QROWS, HEAD), NEG, jnp.float32)
-        mx = score(own, own, mx, False)
-        if own:
-            mx = lax.fori_loop(0, own, lambda i, cur: score(own, i, cur, True), mx)
-        top = jnp.broadcast_to(jnp.max(mx, axis=1, keepdims=True) * LOG2_SCALE, (QROWS, HEAD))
-        total = lax.fori_loop(
-            0, own + 1, lambda i, cur: weigh(i, top, cur), jnp.zeros((QROWS, 2 * HEAD), jnp.float32))
+    def olders(own, start, stop):
+        lax.fori_loop(start, stop, lambda i, cur: score(own, i, True) or cur, 0)
+
+    issue(K)
+    issue(V)
+    issue(Q)
+
+    k0, k1, k2, k3 = [(x + NX - i) % NX for i in range(NX)]
+    share(K, k0)
+    share(K, k1)
+    forward(K, k0)
+    share(K, k2)
+    forward(K, k1)
+    share(K, k3)
+    forward(K, k2)
+    finish(K, k0)
+    forward(K, k3)
+    share(V, 0)
+    finish(K, k1)
+    finish(K, k2)
+    share(V, 1)
+    finish(K, k3)
+    share(V, 2)
+    share(V, 3)
+    for span in range(SPANS):
+        collect(K, span)
+    forward(V, 0)
+
+    def outputs(own, last=None):
+        top = jnp.broadcast_to(jnp.max(peak[own], axis=1, keepdims=True) * LOG2_SCALE, (QROWS, HEAD))
+        total = jnp.zeros((QROWS, 2 * HEAD), jnp.float32)
+        if last is None:
+            total = lax.fori_loop(0, own + 1, lambda i, cur: weigh(own, i, top, cur), total)
+        else:
+            total = lax.fori_loop(0, own, lambda i, cur: weigh(own, i, top, cur), total)
+            last()
+            total = weigh(own, own, top, total)
         result = (total[:, :HEAD] / total[:, HEAD:]).astype(jnp.bfloat16)
         mine[own] = result.reshape(NZ, ROWS, HEAD)
         for dz in range(1, NZ):
@@ -186,6 +204,31 @@
         @pl.when(x == own)
         def _():
             pltpu.make_async_copy(mine.at[own, z], merged.at[:, cols(head)], o_recv).start()
+
+    for own in range(SPANS):
+        arrived(Q, own)
+    score(0, 0, False)
+    forward(V, 1)
+    score(1, 1, False)
+    finish(V, 0)
+    forward(V, 2)
+    olders(1, 0, 1)
+    collect(V, 0)
+    outputs(0)
+    finish(V, 1)
+    forward(V, 3)
+    score(2, 2, False)
+    collect(V, 1)
+    outputs(1)
+    finish(V, 2)
+    olders(2, 0, 1)
+    finish(V, 3)
+    olders(2, 1, 2)
+    collect(V, 2)
+    outputs(2)
+    score(3, 3, False)
+    olders(3, 0, 3)
+    outputs(3, lambda: collect(V, 3))
 
     row = gate[pl.ds(levels[0], 1), :]
     pltpu.make_async_copy(merged, merged, o_recv).wait()
@@ -196,7 +239,7 @@
     for arr in (K, V, Q):
         part = srcs[arr].at[:, pl.ds(0, FEATURES - HEAD)]
         pltpu.make_async_copy(part, part, a2a_send.at[arr]).wait()
-    for arr, span in todo:
+    for arr, span in [(arr, span) for arr in (K, V) for span in range(SPANS)]:
         for kind, zs in enumerate((whole, whole, low, high)):
             y_copy(arr, span, zs, me, up, kind).wait_send()
         for kind, zs in enumerate((whole, whole, whole, low, high)):
@@ -218,7 +261,8 @@
             pltpu.VMEM((SPANS, NZ, NY * 2, ROWS, HEAD), bf16),
             pltpu.VMEM((SPANS, NZ, NY * 2, ROWS, 2 * HEAD), bf16),
             pltpu.VMEM((SPANS, NZ, ROWS, HEAD), bf16),
-            pltpu.VMEM((SPANS * FRAMES, QROWS, HEAD), jnp.float32),
+            pltpu.VMEM((10 * FRAMES, QROWS, HEAD), jnp.float32),
+            pltpu.VMEM((SPANS, QROWS, HEAD), jnp.float32),
             pltpu.VMEM((SPANS, NZ, ROWS, HEAD), bf16),
             pltpu.VMEM((ROWS, FEATURES), bf16),
             dma((3,)),
@@ -231,7 +275,7 @@
             dma,
         ],
         compiler_params=pltpu.CompilerParams(
-            collective_id=0, has_side_effects=True, vmem_limit_bytes=56 * 2**20
+            collective_id=0, has_side_effects=True, vmem_limit_bytes=63 * 2**20
         ),
     )(levels, frame_mask, query_states[0], key_states[0], value_states[0], gate_table)
     return result[None]

time: 77.9 us -> 71.6 us (0.919); the launches traced: 76.9 us -> 71.5 us
  Pallas kernels: 74.5 us -> 69.1 us
    pallas_call x1, Pallas kernels: 74.5 us -> 69.1 us  [on_device(): pl.pallas_call(body, out_shape=jax.ShapeDtypeStruct((ROWS, FEATURES), bf1...]
where the time goes in v1:
time: 71.6 us; the launch traced here: 71.5 us
  Pallas kernels  69.1 us (97%)
  local copies, waits for them, and re-layouts  1.77 us (2%)
    pallas_call x1, Pallas kernels, on_device(): pl.pallas_call(body, out_shape=jax.ShapeDtypeStruct((ROWS, FEATURES), bf1...  69.1 us
    unnamed x1, local copies, waits for them, and re-layouts  1.77 us

profile of v1, /device:TPU:6, one launch (start us, length us, event | category | flops | bytes accessed | tf_op | source)
XLA Modules:
  0.0 71.5 jit_solution(10153376101301217954)
XLA Ops:
  0.7 69.1 %shard_map.64 = bf16[48,4096]{1,0:T(8,128)(2,1)} custom-call(s32[1]{0:T(128)S(6)} %copy.8.levels, s32[4,96]{1,0:T(4,128)} %mask.1, bf16[48,4096]{1,0:T(8,128)(2,1)} %bitcast.5, bf16[48,4096]{1,0:T(8,128)(2,1)} %bitcast.6, bf16[48,4096]{1,0:T(8,128)(2,1)} %bitcast.7, f32[16,4096]{1,0:T(8,128)} %gate.1), custom_call_target="tpu_custom_call" | custom-call | tf_op jit(solution)/shard_map/pallas_call | solution.py:255
  69.7 1.8 %copy.9 = bf16[1,48,4096]{2,1,0:T(8,128)(2,1)} copy(bf16[1,48,4096]{2,1,0:T(8,128)(2,1)} %bitcast.4) | data formatting | bytes 786432

commit v2 on v1

--- a/solution.py
+++ b/solution.py
@@ -22,8 +22,8 @@
 
 
 def body(
-    levels, mask, q_in, k_in, v_in, gate, out,
-    kbuf, vbuf, qbuf, sbuf, peak, mine, merged,
+    mask, q_in, k_in, v_in, merged,
+    kbuf, vbuf, qbuf, sbuf, peak, mine,
     a2a_send, a2a_recv, y_send, y_recv, c_send, c_recv, o_send, o_recv,
 ):
     x = lax.axis_index("span")
@@ -220,19 +220,17 @@
     score(2, 2, False)
     collect(V, 1)
     outputs(1)
+    olders(2, 0, 1)
     finish(V, 2)
-    olders(2, 0, 1)
+    olders(2, 1, 2)
+    score(3, 3, False)
     finish(V, 3)
-    olders(2, 1, 2)
     collect(V, 2)
     outputs(2)
-    score(3, 3, False)
     olders(3, 0, 3)
     outputs(3, lambda: collect(V, 3))
 
-    row = gate[pl.ds(levels[0], 1), :]
     pltpu.make_async_copy(merged, merged, o_recv).wait()
-    out[...] = (row * merged[...].astype(jnp.float32)).astype(jnp.bfloat16)
 
     part = merged.at[:, pl.ds(0, FEATURES - HEAD)]
     pltpu.make_async_copy(part, part, o_send).wait()
@@ -255,8 +253,8 @@
     result = pl.pallas_call(
         body,
         out_shape=jax.ShapeDtypeStruct((ROWS, FEATURES), bf16),
-        in_specs=[smem, smem, hbm, hbm, hbm, vmem],
-        out_specs=vmem,
+        in_specs=[smem, hbm, hbm, hbm],
+        out_specs=hbm,
         scratch_shapes=[
             pltpu.VMEM((SPANS, NZ, NY * 2, ROWS, HEAD), bf16),
             pltpu.VMEM((SPANS, NZ, NY * 2, ROWS, 2 * HEAD), bf16),
@@ -264,7 +262,6 @@
             pltpu.VMEM((10 * FRAMES, QROWS, HEAD), jnp.float32),
             pltpu.VMEM((SPANS, QROWS, HEAD), jnp.float32),
             pltpu.VMEM((SPANS, NZ, ROWS, HEAD), bf16),
-            pltpu.VMEM((ROWS, FEATURES), bf16),
             dma((3,)),
             dma((3, SPANS)),
             dma((2, SPANS, 4)),
@@ -277,8 +274,9 @@
         compiler_params=pltpu.CompilerParams(
             collective_id=0, has_side_effects=True, vmem_limit_bytes=63 * 2**20
         ),
-    )(levels, frame_mask, query_states[0], key_states[0], value_states[0], gate_table)
-    return result[None]
+    )(frame_mask, query_states[0], key_states[0], value_states[0])
+    row = lax.dynamic_slice_in_dim(gate_table, levels[0], 1, axis=0)
+    return (row * result.astype(jnp.float32)).astype(bf16)[None]
 
 
 def solution(mesh):

time: 71.6 us -> 70.7 us (0.987)
  other arithmetic: 0 us -> 1.81 us
  local copies, waits for them, and re-layouts: 1.77 us -> 0.28 us
  Pallas kernels: 69.1 us -> 67.7 us
    broadcast_in_dim x0 -> x1, other arithmetic: none -> 1.81 us  [on_device(): return (row * result.astype(jnp.float32)).astype(bf16)[None]]
    unnamed x1 -> x2, local copies, waits for them, and re-layouts: 1.77 us -> 0.27 us
    pallas_call x1, Pallas kernels: 69.1 us -> 67.7 us  [on_device(): pl.pallas_call(body, out_shape=jax.ShapeDtypeStruct((ROWS, FEATURES), bf1...]
where the time goes in v2:
time: 70.7 us; the launch traced here: 70.5 us
  Pallas kernels  67.7 us (96%)
  other arithmetic  1.81 us (3%)
  between operations  0.71 us (1%)
    pallas_call x1, Pallas kernels, on_device(): pl.pallas_call(body, out_shape=jax.ShapeDtypeStruct((ROWS, FEATURES), bf1...  67.7 us
    broadcast_in_dim x1, other arithmetic, on_device(): return (row * result.astype(jnp.float32)).astype(bf16)[None]  1.81 us

profile of v2, /device:TPU:6, one launch (start us, length us, event | category | flops | bytes accessed | tf_op | source)
XLA Modules:
  0.0 70.5 jit_solution(326246785119177117)
XLA Ops:
  0.0 0.0 copy-start
  0.7 0.3 copy-done
  1.0 67.7 %shard_map.64 = bf16[48,4096]{1,0:T(8,128)(2,1)} custom-call(s32[4,96]{1,0:T(4,128)} %mask.1, bf16[48,4096]{1,0:T(8,128)(2,1)} %bitcast.10, bf16[48,4096]{1,0:T(8,128)(2,1)} %bitcast.11, bf16[48,4096]{1,0:T(8,128)(2,1)} %bitcast.12), custom_call_target="tpu_custom_call" | custom-call | tf_op jit(solution)/shard_map/pallas_call | solution.py:253
  68.7 1.8 %fusion = bf16[1,48,4096]{2,1,0:T(8,128)(2,1)} fusion(bf16[48,4096]{1,0:T(8,128)(2,1)} %shard_map.64, f32[4096]{0:T(1024)S(1)} %bitcast.13), kind=kLoop, calls=%fused_computation.1 | loop fusion | flops 589824 | bytes 802816 | tf_op jit(solution)/shard_map/broadcast_in_dim | solution.py:279
  (1 shorter events, 0.0 us)
Async XLA Ops:
  0.0 1.0 %copy-start = (f32[16,4096]{1,0:T(8,128)S(1)}, f32[16,4096]{1,0:T(8,128)}, u32[]{:S(2)}) copy-start(f32[16,4096]{1,0:T(8,128)} %param.11) | copy-start | bytes 786436

commit v3 on v2

--- a/solution.py
+++ b/solution.py
@@ -225,9 +225,9 @@
     olders(2, 1, 2)
     score(3, 3, False)
     finish(V, 3)
+    olders(3, 0, 3)
     collect(V, 2)
     outputs(2)
-    olders(3, 0, 3)
     outputs(3, lambda: collect(V, 3))
 
     pltpu.make_async_copy(merged, merged, o_recv).wait()

time: 70.7 us -> 70.7 us (level)
  no operation moved by 1% of the time
where the time goes in v3:
time: 70.7 us; the launch traced here: 70.5 us
  Pallas kernels  67.7 us (96%)
  other arithmetic  1.81 us (3%)
  between operations  0.71 us (1%)
    pallas_call x1, Pallas kernels, on_device(): pl.pallas_call(body, out_shape=jax.ShapeDtypeStruct((ROWS, FEATURES), bf1...  67.7 us
    broadcast_in_dim x1, other arithmetic, on_device(): return (row * result.astype(jnp.float32)).astype(bf16)[None]  1.81 us

profile of v3, /device:TPU:6, one launch (start us, length us, event | category | flops | bytes accessed | tf_op | source)
XLA Modules:
  0.0 70.5 jit_solution(9166726812512377059)
XLA Ops:
  0.0 0.0 copy-start
  0.7 0.3 copy-done
  1.0 67.7 %shard_map.64 = bf16[48,4096]{1,0:T(8,128)(2,1)} custom-call(s32[4,96]{1,0:T(4,128)} %mask.1, bf16[48,4096]{1,0:T(8,128)(2,1)} %bitcast.10, bf16[48,4096]{1,0:T(8,128)(2,1)} %bitcast.11, bf16[48,4096]{1,0:T(8,128)(2,1)} %bitcast.12), custom_call_target="tpu_custom_call" | custom-call | tf_op jit(solution)/shard_map/pallas_call | solution.py:253
  68.7 1.8 %fusion = bf16[1,48,4096]{2,1,0:T(8,128)(2,1)} fusion(bf16[48,4096]{1,0:T(8,128)(2,1)} %shard_map.64, f32[4096]{0:T(1024)S(1)} %bitcast.13), kind=kLoop, calls=%fused_computation.1 | loop fusion | flops 589824 | bytes 802816 | tf_op jit(solution)/shard_map/broadcast_in_dim | solution.py:279
  (1 shorter events, 0.0 us)
Async XLA Ops:
  0.0 1.0 %copy-start = (f32[16,4096]{1,0:T(8,128)S(1)}, f32[16,4096]{1,0:T(8,128)}, u32[]{:S(2)}) copy-start(f32[16,4096]{1,0:T(8,128)} %param.11) | copy-start | bytes 786436
